TPU v7x, 256 devices: a whole 4x4x8 slice. The times are simulated.
256 devices in a mesh: row: 16 (over x_lo, y, core), col: 16 (over x_hi, z).
Axes of the slice: x: 4 (x_hi: 2, x_lo: 2; x = x_hi * 2 + x_lo), y: 4, z: 8, core: 2. Of those that a mesh axis runs over, the one named last changes fastest.
Arguments:
- pair_act: bfloat16 [512, 512, 128], P('row', 'col'), may hold values from -6 to 6
- norm_gain: float32 [128], replicated, may hold values from 0.1 to 1.9
- norm_bias: float32 [128], replicated, may hold values from -3 to 3
- proj_weight: bfloat16 [128, 512], replicated, may hold values from -0.5 to 0.5
- proj_bias: float32 [512], replicated, may hold values from -3 to 3
- gate_weight: bfloat16 [128, 128], replicated, may hold values from -0.5 to 0.5
- gate_bias: float32 [128], replicated, may hold values from -3 to 3
- mid_gain: float32 [128], replicated, may hold values from 0.1 to 1.9
- mid_bias: float32 [128], replicated, may hold values from -3 to 3
- out_weight: bfloat16 [128, 128], replicated, may hold values from -0.5 to 0.5
- out_bias: float32 [128], replicated, may hold values from -3 to 3
Outputs:
- update: bfloat16 [512, 512, 128], P('row', 'col')
All inputs are finite; a program needn't handle non-finite values.
Results may differ from a plain program's by a relative error of at most 0.0051.
Values may be sent and summed in bfloat16 or wider, within the bound.
A program may use at most 128 MiB of HBM per device.

v0:
```python
import jax
import jax.numpy as jnp
from jax import lax
from jax.sharding import PartitionSpec as P


def from_root(array, axis, root):
    mine = lax.axis_index(axis) == root
    return lax.psum(jnp.where(mine, array, jnp.zeros_like(array)), axis)


def layer_norm(values, scale_vec, shift_vec):
    center = values - jnp.mean(values, axis=-1, keepdims=True)
    spread = jnp.mean(center * center, axis=-1, keepdims=True)
    return center * lax.rsqrt(spread + 1e-05) * scale_vec + shift_vec


def per_device(
    pair_act,
    norm_gain,
    norm_bias,
    proj_weight,
    proj_bias,
    gate_weight,
    gate_bias,
    mid_gain,
    mid_bias,
    out_weight,
    out_bias,
):
    row_width, col_width, chan_count = pair_act.shape
    hid_count = out_weight.shape[0]
    row_count = lax.axis_size("row")
    col_count = lax.axis_size("col")
    normed = layer_norm(pair_act.astype(jnp.float32), norm_gain, norm_bias).astype(jnp.bfloat16)
    flat_norm = normed.reshape(row_width * col_width, chan_count)
    projected = jnp.dot(flat_norm, proj_weight, preferred_element_type=jnp.float32) + proj_bias
    left_proj = (
        (jax.nn.sigmoid(projected[:, :hid_count]) * projected[:, hid_count : 2 * hid_count])
        .astype(jnp.bfloat16)
        .reshape(row_width, col_width, hid_count)
    )
    right_proj = (
        (
            jax.nn.sigmoid(projected[:, 2 * hid_count : 3 * hid_count])
            * projected[:, 3 * hid_count :]
        )
        .astype(jnp.bfloat16)
        .reshape(row_width, col_width, hid_count)
    )
    gate_value = jax.nn.sigmoid(
        jnp.dot(flat_norm, gate_weight, preferred_element_type=jnp.float32) + gate_bias
    )
    left_band, right_band = (
        lax.all_gather(left_proj, "row", axis=0, tiled=True),
        lax.all_gather(right_proj, "row", axis=0, tiled=True),
    )
    group_ratio = row_count // col_count
    row_place = lax.axis_index("row")
    left_panel = from_root(left_band, "col", row_place // group_ratio)
    mixed_sum = jnp.einsum(
        "kih,kjh->ijh", left_panel, right_band, preferred_element_type=jnp.float32
    )
    hidden_norm = (
        layer_norm(mixed_sum, mid_gain, mid_bias)
        .astype(jnp.bfloat16)
        .reshape(row_width * col_width, hid_count)
    )
    outcome = jnp.dot(hidden_norm, out_weight, preferred_element_type=jnp.float32) + out_bias
    return (gate_value * outcome).astype(jnp.bfloat16).reshape(row_width, col_width, chan_count)


def solution(mesh):
    placed = (P("row", "col", None), P(), P(), P(), P(), P(), P(), P(), P(), P(), P())
    return jax.shard_map(
        per_device, mesh=mesh, in_specs=placed, out_specs=P("row", "col", None), check_vma=False
    )
```

profile of v0, /device:TPU:8, one launch (start us, length us, event | category | flops | bytes accessed | tf_op | source)
XLA Modules:
  0.0 289.3 jit_solution(13438229588797291751)
XLA Ops:
  6.5 0.0 copy-start
  6.5 0.0 all-gather.5.cloned.1.call-start
  6.5 1.2 convert_reduce_fusion
  7.7 1.3 fusion.8
  9.1 1.3 fusion.11
  10.4 0.0 copy-done
  10.4 1.1 convolution_add_fusion
  11.5 1.1 fusion.12
  12.6 0.0 all-gather.5.cloned.1.call-update
  12.6 0.0 all-gather.3.cloned.1.call-start
  12.7 0.7 all-gather.3.cloned.1.call-update
  13.4 0.0 all-reduce.2.cloned.1.call-start
  13.4 41.8 %all-gather.5.cloned.1.call-done = bf16[512,32,128]{2,1,0:T(8,128)(2,1)} async-done(((bf16[32,32,128]{2,1,0:T(8,128)(2,1)}), bf16[512,32,128]{2,1,0:T(8,128)(2,1)}) %all-gather.5.cloned.1.call-update) | async-done | bytes 4194320 | tf_op jit(solution)/shard_map/all_gather | solution.py:55
  55.3 8.6 %copy.33 = bf16[512,32,128]{0,1,2:T(8,128)(2,1)} copy(bf16[512,32,128]{2,1,0:T(8,128)(2,1)} %all-gather.5.cloned.1.call-done) | data formatting | bytes 8388608 | tf_op jit(solution)/shard_map/all_gather | solution.py:55
  63.9 2.2 broadcast_select_fusion
  66.1 0.0 all-reduce.2.cloned.1.call-update
  66.1 31.0 %all-gather.3.cloned.1.call-done = bf16[512,32,128]{2,1,0:T(8,128)(2,1)} async-done(((bf16[32,32,128]{2,1,0:T(8,128)(2,1)}), bf16[512,32,128]{2,1,0:T(8,128)(2,1)}) %all-gather.3.cloned.1.call-update) | async-done | bytes 4194320 | tf_op jit(solution)/shard_map/all_gather | solution.py:56
  97.1 8.5 %copy.34 = bf16[512,32,128]{0,1,2:T(8,128)(2,1)} copy(bf16[512,32,128]{2,1,0:T(8,128)(2,1)} %all-gather.3.cloned.1.call-done) | data formatting | bytes 8388608 | tf_op jit(solution)/shard_map/all_gather | solution.py:56
  105.7 0.0 copy-start.2
  105.7 0.0 copy-start.3
  105.7 0.0 copy-start.1
  105.7 0.0 copy-start.4
  105.7 168.8 %all-reduce.2.cloned.1.call-done = bf16[512,32,128]{0,1,2:T(8,128)(2,1)} async-done(((bf16[512,32,128]{0,1,2:T(8,128)(2,1)}), bf16[512,32,128]{0,1,2:T(8,128)(2,1)}) %all-reduce.2.cloned.1.call-update) | async-done | bytes 4194320 | tf_op jit(solution)/shard_map/psum | solution.py:9
  274.5 4.7 %bitcast_reduce_fusion = (f32[32,32]{0,1:T(8,128)S(1)}, f32[128,32,32]{2,1,0:T(8,128)S(1)}) fusion(bf16[512,32,128]{0,1,2:T(8,128)(2,1)} %copy.34, bf16[512,32,128]{0,1,2:T(8,128)(2,1)} %all-reduce.2.cloned.1.call-done), kind=kOutput, calls=%fused_computation.1 | convolution fusion | flops 134347776 | bytes 8916992 | tf_op jit(solution)/shard_map/kih,kjh->ijh/dot_general | solution.py:61
  279.2 0.0 copy-start.5
  279.2 0.0 copy-start.6
  279.2 1.4 copy.35
  280.6 0.1 copy.37
  280.7 0.4 multiply_reduce_fusion
  281.1 0.0 copy-done.2
  281.1 0.0 copy-done.3
  281.2 0.3 add_convert_fusion
  281.5 0.0 copy-done.1
  281.5 0.0 copy-done.4
  281.5 0.2 convolution_add_fusion.1
  281.7 0.0 copy-done.5
  281.7 0.0 copy-done.6
  281.8 1.0 fusion.5
  (4 shorter events, 0.0 us)
Async XLA Ops:
  6.5 3.9 %copy-start = (bf16[128,512]{1,0:T(8,128)(2,1)S(1)}, bf16[128,512]{1,0:T(8,128)(2,1)}, u32[]{:S(2)}) copy-start(bf16[128,512]{1,0:T(8,128)(2,1)} %param.14) | copy-start | bytes 393220
  6.5 48.7 %all-gather.5.cloned.1.call-start = ((), (), s32[]{:S(2)}) async-start(), calls=%async_computation.1 | async-start | bytes 4456448 | tf_op jit(solution)/shard_map/all_gather | solution.py:55
  12.6 84.5 %all-gather.3.cloned.1.call-start = ((), (), s32[]{:S(2)}) async-start(), calls=%async_computation | async-start | bytes 4456448 | tf_op jit(solution)/shard_map/all_gather | solution.py:56
  13.4 261.1 %all-reduce.2.cloned.1.call-start = ((), (), s32[]{:S(2)}) async-start(), calls=%async_computation.2 | async-start | bytes 8388608 | tf_op jit(solution)/shard_map/psum | solution.py:9
  105.7 175.4 %copy-start.2 = (f32[128]{0:T(128)S(1)}, f32[128]{0:T(128)}, u32[]{:S(2)}) copy-start(f32[128]{0:T(128)} %param.19) | copy-start | bytes 1540
  105.7 175.5 %copy-start.3 = (f32[128]{0:T(128)S(1)}, f32[128]{0:T(128)}, u32[]{:S(2)}) copy-start(f32[128]{0:T(128)} %param.18) | copy-start | bytes 1540
  105.7 175.8 %copy-start.1 = (bf16[128,128]{1,0:T(8,128)(2,1)S(1)}, bf16[128,128]{1,0:T(8,128)(2,1)}, u32[]{:S(2)}) copy-start(bf16[128,128]{1,0:T(8,128)(2,1)} %param.20) | copy-start | bytes 98308
  105.7 175.8 %copy-start.4 = (f32[128]{0:T(128)S(1)}, f32[128]{0:T(128)}, u32[]{:S(2)}) copy-start(f32[128]{0:T(128)} %param.21) | copy-start | bytes 1540
  279.2 2.5 copy-start.5
  279.2 2.5 copy-start.6
Sparse Core Ops, SparseCore 0:
  12.8 42.4 all-gather.4
  57.1 39.9 all-gather.2
  99.8 174.6 all-reduce.1
where the time goes:
time: 290 us; the launch traced here: 289 us
  waiting for transfers between devices  242 us (83%)
  local copies, waits for them, and re-layouts  18.7 us (6%)
  between operations  13.3 us (5%)
  other arithmetic  7.89 us (3%)
  matrix products  6.99 us (2%)
    psum x1, waiting for transfers between devices, from_root(): return lax.psum(jnp.where(mine, array, jnp.zeros_like(array)), axis)  169 us
    all_gather x1, waiting for transfers between devices, per_device(): lax.all_gather(left_proj, 'row', axis=0, tiled=True)  41.8 us
    all_gather x1, waiting for transfers between devices, per_device(): lax.all_gather(right_proj, 'row', axis=0, tiled=True)  31 us
    all_gather x1, local copies, waits for them, and re-layouts, per_device(): lax.all_gather(left_proj, 'row', axis=0, tiled=True)  8.62 us
    all_gather x1, local copies, waits for them, and re-layouts, per_device(): lax.all_gather(right_proj, 'row', axis=0, tiled=True)  8.54 us
  transfers between devices with their start and end apart: 3, of which 3 were waited for; matrix products, arithmetic and copies ran while one was open for 7% of the time, Pallas kernels for 0%

commit v1 on v0

v1 whole, which is shorter than its diff:
```python
import jax
import jax.numpy as jnp
from jax import lax
from jax.experimental import pallas as pl
from jax.experimental.pallas import tpu as pltpu
from jax.sharding import PartitionSpec as P

MESH = pl.DeviceIdType.MESH
BF16 = jnp.bfloat16
F32 = jnp.float32
EPS = 1e-05

NX, NY, NZ = 4, 4, 8
CHIPS = NX * NY * NZ


def place():
    row, col = lax.axis_index("row"), lax.axis_index("col")
    core = lax.rem(row, 2)
    y = lax.rem(lax.div(row, 2), NY)
    x = lax.div(col, NZ) * 2 + lax.div(row, 2 * NY)
    return x, y, lax.rem(col, NZ), core


def device(x, y, z, core):
    return lax.rem(x, 2) * 8 + y * 2 + core, lax.div(x, 2) * NZ + z


def transpose_blocks(v, lane):
    low, even = lane < 64, lax.rem(lax.div(lane, 32), 2) == 0
    u0 = jnp.where(low, v[0], pltpu.roll(v[2], 64, 1))
    u2 = jnp.where(low, pltpu.roll(v[0], 64, 1), v[2])
    u1 = jnp.where(low, v[1], pltpu.roll(v[3], 64, 1))
    u3 = jnp.where(low, pltpu.roll(v[1], 64, 1), v[3])
    return (
        jnp.where(even, u0, pltpu.roll(u1, 32, 1)),
        jnp.where(even, pltpu.roll(u0, 96, 1), u1),
        jnp.where(even, u2, pltpu.roll(u3, 32, 1)),
        jnp.where(even, pltpu.roll(u2, 96, 1), u3),
    )


def column(vec, width):
    return jnp.transpose(jnp.broadcast_to(vec, (width, vec.shape[1])))


def kernel(
    x_ref, ng_ref, nb_ref, pw_ref, pb_ref, gw_ref, gb_ref, mg_ref, mb_ref, ow_ref, ob_ref,
    out_ref,
    xn, wt, pbt, grp, send, recv, left, right, part, part_in, total, back, back_in, mixed, gate,
    mgt, mbt, send_sem, recv_sem, part_send, part_recv, back_send, back_recv,
):
    x, y, z, core = place()
    rows, cols = device(x, y, z, core)
    slot = lax.div(rows, 2) * 16 + cols
    chan = (x * NY + y) * NZ + z
    partner = device(x, y, z, 1 - core)

    barrier = pltpu.get_barrier_semaphore()

    def greet(i, carry):
        dx, dy, dz = lax.div(i, 32), lax.rem(lax.div(i, 8), 4), lax.rem(i, 8)
        peer = device(lax.rem(x + dx, NX), lax.rem(y + dy, NY), lax.rem(z + dz, NZ), core)
        pl.semaphore_signal(barrier, inc=1, device_id=peer, device_id_type=MESH)
        return carry

    lax.fori_loop(1, CHIPS, greet, 0)
    pl.semaphore_signal(barrier, inc=1, device_id=partner, device_id_type=MESH)

    for t in range(8):
        chunk = pl.ds(t * 128, 128)
        v = x_ref[chunk, :].astype(F32)
        center = v - jnp.mean(v, axis=1, keepdims=True)
        spread = jnp.mean(center * center, axis=1, keepdims=True)
        xn[chunk, :] = (center * lax.rsqrt(spread + EPS) * ng_ref[...] + nb_ref[...]).astype(BF16)
    for t in range(4):
        wt[pl.ds(t * 128, 128), :] = jnp.transpose(pw_ref[:, t * 128 : (t + 1) * 128])
        pbt[pl.ds(t * 128, 128), :] = column(pb_ref[:, t * 128 : (t + 1) * 128], 128)

    pl.semaphore_wait(barrier, CHIPS)

    def project(i, carry):
        group = lax.rem(x * 2 + lax.div(y, 2) + 1 + i, 8)
        first = pl.multiple_of(group * 16, 16)
        weight = jnp.concatenate([wt[pl.ds(b * 128 + first, 16), :] for b in range(4)], axis=0)
        bias = [pbt[pl.ds(b * 128 + first, 16), :] for b in range(4)]
        for half in range(2):
            proj = lax.dot_general(
                weight,
                xn[pl.ds(half * 512, 512), :],
                (((1,), (1,)), ((), ())),
                preferred_element_type=F32,
            )
            for s in range(4):
                t = half * 4 + s
                p = [
                    proj[b * 16 : (b + 1) * 16, s * 128 : (s + 1) * 128] + bias[b]
                    for b in range(4)
                ]
                grp[pl.ds(t, 16, stride=16), :] = jax.nn.sigmoid(p[0]) * p[1]
                grp[pl.ds(8 + t, 16, stride=16), :] = jax.nn.sigmoid(p[2]) * p[3]
        send[pl.ds(first, 16)] = grp[...].reshape(16, 16, 128).astype(BF16)
        tx = lax.div(group, 2)
        for dy in range(2):
            ty = lax.rem(group, 2) * 2 + dy
            for dz in range(8):
                tz = lax.rem(z + dz, NZ)
                target = (tx * NY + ty) * NZ + tz

                def push(tx=tx, ty=ty, tz=tz, target=target):
                    pltpu.make_async_remote_copy(
                        src_ref=send.at[target],
                        dst_ref=recv.at[slot],
                        send_sem=send_sem,
                        recv_sem=recv_sem,
                        device_id=device(tx, ty, tz, core),
                        device_id_type=MESH,
                    ).start()

                if dz == 0:
                    pl.when(target != chan)(push)
                else:
                    push()
        return carry

    lax.fori_loop(0, 8, project, 0)
    recv[slot] = send[chan]

    for t in range(8):
        chunk = pl.ds(t * 128, 128)
        gate[chunk, :] = jax.nn.sigmoid(
            jnp.dot(xn[chunk, :], gw_ref[...], preferred_element_type=F32) + gb_ref[...]
        )
    mgt[...] = column(mg_ref[...], 128)
    mbt[...] = column(mb_ref[...], 128)

    sent = send.at[pl.ds(0, CHIPS - 1)]
    landed = recv.at[pl.ds(0, CHIPS - 1)]
    pltpu.make_async_copy(landed, landed, recv_sem).wait()

    lane = lax.broadcasted_iota(jnp.int32, (16, 128), 1)
    for p in range(4):
        for g in range(4):
            cs = [(g % 2) * 8 + 2 * m + g // 2 for m in range(4)]
            both = [
                [recv[(2 * p + q) * 16 + c].astype(F32) for q in range(2)] for c in cs
            ]
            for side, store in ((0, left), (8, right)):
                tiles = [
                    jnp.concatenate([one[side : side + 8] for one in pair], axis=0)
                    for pair in both
                ]
                for k4, tile in enumerate(transpose_blocks(tiles, lane)):
                    store[pl.ds(k4 * 64 + p * 16, 16), pl.ds(g * 128, 128)] = tile.astype(BF16)

    def product(which):
        start = pl.multiple_of(which * 256, 256)
        return lax.dot_general(
            left[:, pl.ds(start, 256)],
            right[...],
            (((0,), (0,)), ((), ())),
            preferred_element_type=F32,
        )

    part[...] = product(1 - core)
    swap = pltpu.make_async_remote_copy(
        src_ref=part,
        dst_ref=part_in,
        send_sem=part_send,
        recv_sem=part_recv,
        device_id=partner,
        device_id_type=MESH,
    )
    swap.start()
    total[...] = product(core)
    swap.wait_recv()

    lane8 = lax.broadcasted_iota(jnp.int32, (8, 128), 1)

    def give(i, carry):
        par = lax.rem(lax.rem(z, 2) + lax.div(i, 16), 2)
        tx = lax.rem(x + lax.div(lax.rem(i, 16), 4), NX)
        ty = lax.rem(y + lax.rem(i, 4), NY)
        b = lax.rem(tx, 2) * NY + ty
        g = par * 2 + lax.div(tx, 2)
        lanes = pl.ds(pl.multiple_of(g * 128, 128), 128)
        tiles = []
        for q in range(4):
            here = (pl.ds(pl.multiple_of(b * 32 + q * 8, 8), 8), lanes)
            tiles.append(total[here] + part_in[here])
        for m, tile in enumerate(transpose_blocks(tiles, lane8)):
            tz = 2 * m + par
            target = (tx * NY + ty) * NZ + tz
            back[target] = tile.astype(BF16)

            @pl.when(target != chan)
            def _(tz=tz, target=target):
                pltpu.make_async_remote_copy(
                    src_ref=back.at[target],
                    dst_ref=back_in.at[chan],
                    send_sem=back_send,
                    recv_sem=back_recv,
                    device_id=device(tx, ty, tz, core),
                    device_id_type=MESH,
                ).start()

        return carry

    lax.fori_loop(0, 32, give, 0)
    back_in[chan] = back[chan]

    gone = back.at[pl.ds(0, CHIPS - 1)]
    came = back_in.at[pl.ds(0, CHIPS - 1)]
    pltpu.make_async_copy(came, came, back_recv).wait()

    values = back_in[...].astype(F32)
    center = values - jnp.mean(values, axis=0, keepdims=True)
    spread = jnp.mean(center * center, axis=0, keepdims=True)
    mixed[...] = (center * lax.rsqrt(spread + EPS)).reshape(1024, 128)
    for t in range(8):
        norm = mixed[pl.ds(t, 128, stride=8), :] * mgt[...] + mbt[...]
        res = lax.dot_general(
            norm.astype(BF16),
            ow_ref[...],
            (((0,), (0,)), ((), ())),
            preferred_element_type=F32,
        ) + ob_ref[...]
        for q in range(4):
            where = pl.ds(q * 256 + t * 32, 32)
            out_ref[where, :] = (gate[where, :] * res[q * 32 : (q + 1) * 32]).astype(BF16)

    pltpu.make_async_copy(sent, sent, send_sem).wait()
    swap.wait_send()
    pltpu.make_async_copy(gone, gone, back_send).wait()


def per_device(
    pair_act, norm_gain, norm_bias, proj_weight, proj_bias, gate_weight, gate_bias, mid_gain,
    mid_bias, out_weight, out_bias,
):
    dma = pltpu.SemaphoreType.DMA
    vmem = pltpu.VMEM
    out = pl.pallas_call(
        kernel,
        out_shape=jax.ShapeDtypeStruct((1024, 128), BF16),
        in_specs=[pl.BlockSpec(memory_space=vmem)] * 11,
        out_specs=pl.BlockSpec(memory_space=vmem),
        scratch_shapes=[
            vmem((1024, 128), BF16),
            vmem((512, 128), BF16),
            vmem((512, 128), F32),
            vmem((256, 128), F32),
            vmem((CHIPS, 16, 128), BF16),
            vmem((CHIPS, 16, 128), BF16),
            vmem((256, 512), BF16),
            vmem((256, 512), BF16),
            vmem((256, 512), F32),
            vmem((256, 512), F32),
            vmem((256, 512), F32),
            vmem((CHIPS, 8, 128), BF16),
            vmem((CHIPS, 8, 128), BF16),
            vmem((1024, 128), F32),
            vmem((1024, 128), F32),
            vmem((128, 128), F32),
            vmem((128, 128), F32),
            dma, dma, dma, dma, dma, dma,
        ],
        compiler_params=pltpu.CompilerParams(
            collective_id=0, has_side_effects=True, vmem_limit_bytes=40 << 20
        ),
        cost_estimate=pl.CostEstimate(
            flops=500_000_000, bytes_accessed=2_000_000, transcendentals=1_000_000
        ),
        name="triangle",
    )(
        pair_act.reshape(1024, 128),
        norm_gain.reshape(1, -1),
        norm_bias.reshape(1, -1),
        proj_weight,
        proj_bias.reshape(1, -1),
        gate_weight,
        gate_bias.reshape(1, -1),
        mid_gain.reshape(1, -1),
        mid_bias.reshape(1, -1),
        out_weight,
        out_bias.reshape(1, -1),
    )
    return out.reshape(32, 32, 128)


def solution(mesh):
    placed = (P("row", "col", None),) + (P(),) * 10
    return jax.shard_map(
        per_device, mesh=mesh, in_specs=placed, out_specs=P("row", "col", None), check_vma=False
    )
```

time: 290 us -> 48.8 us (0.17)
  the two profiles are of different devices: /device:TPU:8 before, /device:TPU:1 now
where the time goes in v1:
time: 48.8 us; the launch traced here: 48.5 us
  Pallas kernels  43.7 us (90%)
  local copies, waits for them, and re-layouts  4.78 us (10%)
    pallas_call x1, Pallas kernels, per_device(): pl.pallas_call(kernel, out_shape=jax.ShapeDtypeStruct((1024, 128), BF16),...  43.7 us
    unnamed x23, local copies, waits for them, and re-layouts  4.78 us

profile of v1, /device:TPU:1, one launch (start us, length us, event | category | flops | bytes accessed | tf_op | source)
XLA Modules:
  0.0 48.5 jit_solution(4120403785910313682)
XLA Ops:
  0.0 0.0 copy-start.8
  0.0 0.0 copy-start.9
  0.0 0.0 copy-start.10
  0.0 0.0 copy-start.4
  0.0 0.0 copy-start.5
  0.0 0.0 copy-start.6
  0.0 0.0 copy-start.7
  0.0 0.6 %copy-done.8 = f32[128]{0:T(128)S(1)} copy-done((f32[128]{0:T(128)S(1)}, f32[128]{0:T(128)}, u32[]{:S(2)}) %copy-start.8) | copy-done | bytes 536
  0.7 0.0 copy-done.9
  0.7 0.0 copy-done.10
  0.7 0.0 copy-done.4
  0.7 0.0 copy-done.5
  0.7 0.0 copy-done.6
  0.7 0.0 copy-done.7
  0.8 0.0 copy-start
  0.8 0.9 %copy-done = bf16[32,32,128]{2,1,0:T(8,128)(2,1)S(1)} copy-done((bf16[32,32,128]{2,1,0:T(8,128)(2,1)S(1)}, bf16[32,32,128]{2,1,0:T(8,128)(2,1)}, u32[]{:S(2)}) %copy-start) | copy-done | bytes 262168
  1.7 0.0 copy-start.1
  1.7 0.9 %copy-done.1 = bf16[128,512]{1,0:T(8,128)(2,1)S(1)} copy-done((bf16[128,512]{1,0:T(8,128)(2,1)S(1)}, bf16[128,512]{1,0:T(8,128)(2,1)}, u32[]{:S(2)}) %copy-start.1) | copy-done | bytes 131096
  2.6 0.0 copy-start.2
  2.6 0.8 %copy-done.2 = bf16[128,128]{1,0:T(8,128)(2,1)S(1)} copy-done((bf16[128,128]{1,0:T(8,128)(2,1)S(1)}, bf16[128,128]{1,0:T(8,128)(2,1)}, u32[]{:S(2)}) %copy-start.2) | copy-done | bytes 32792
  3.4 0.0 copy-start.3
  3.4 0.8 %copy-done.3 = bf16[128,128]{1,0:T(8,128)(2,1)S(1)} copy-done((bf16[128,128]{1,0:T(8,128)(2,1)S(1)}, bf16[128,128]{1,0:T(8,128)(2,1)}, u32[]{:S(2)}) %copy-start.3) | copy-done | bytes 32792
  4.1 43.7 %triangle.1 = bf16[1024,128]{1,0:T(8,128)(2,1)S(1)} custom-call(bf16[1024,128]{1,0:T(8,128)(2,1)S(1)} %bitcast.10, f32[1,128]{1,0:T(1,128)S(1)} %bitcast.12, f32[1,128]{1,0:T(1,128)S(1)} %bitcast.13, bf16[128,512]{1,0:T(8,128)(2,1)S(1)} %copy-done.1, f32[1,512]{1,0:T(1,128)S(1)} %bitcast.11, bf16[128,128]{1,0:T(8,128)(2,1)S(1)} %copy-done.2, ...), custom_call_target="tpu_custom_call" | custom-call | flops 500000000 | bytes 2000000 | tf_op jit(solution)/shard_map/triangle/pallas_call | solution.py:243
  47.8 0.7 %copy.13 = bf16[32,32,128]{2,1,0:T(8,128)(2,1)} copy(bf16[32,32,128]{2,1,0:T(8,128)(2,1)S(1)} %bitcast.9) | data formatting | bytes 524288
Async XLA Ops:
  0.0 0.7 %copy-start.8 = (f32[128]{0:T(128)S(1)}, f32[128]{0:T(128)}, u32[]{:S(2)}) copy-start(f32[128]{0:T(128)} %param.18) | copy-start | bytes 1540
  0.0 0.7 %copy-start.9 = (f32[128]{0:T(128)S(1)}, f32[128]{0:T(128)}, u32[]{:S(2)}) copy-start(f32[128]{0:T(128)} %param.19) | copy-start | bytes 1540
  0.0 0.7 %copy-start.10 = (f32[128]{0:T(128)S(1)}, f32[128]{0:T(128)}, u32[]{:S(2)}) copy-start(f32[128]{0:T(128)} %param.21) | copy-start | bytes 1540
  0.0 0.7 %copy-start.4 = (f32[512]{0:T(512)S(1)}, f32[512]{0:T(512)}, u32[]{:S(2)}) copy-start(f32[512]{0:T(512)} %param.15) | copy-start | bytes 6148
  0.0 0.7 %copy-start.5 = (f32[128]{0:T(128)S(1)}, f32[128]{0:T(128)}, u32[]{:S(2)}) copy-start(f32[128]{0:T(128)} %param.12) | copy-start | bytes 1540
  0.0 0.7 %copy-start.6 = (f32[128]{0:T(128)S(1)}, f32[128]{0:T(128)}, u32[]{:S(2)}) copy-start(f32[128]{0:T(128)} %param.13) | copy-start | bytes 1540
  0.0 0.7 %copy-start.7 = (f32[128]{0:T(128)S(1)}, f32[128]{0:T(128)}, u32[]{:S(2)}) copy-start(f32[128]{0:T(128)} %param.17) | copy-start | bytes 1540
  0.8 0.9 %copy-start = (bf16[32,32,128]{2,1,0:T(8,128)(2,1)S(1)}, bf16[32,32,128]{2,1,0:T(8,128)(2,1)}, u32[]{:S(2)}) copy-start(bf16[32,32,128]{2,1,0:T(8,128)(2,1)} %param.11) | copy-start | bytes 786436
  1.7 0.9 %copy-start.1 = (bf16[128,512]{1,0:T(8,128)(2,1)S(1)}, bf16[128,512]{1,0:T(8,128)(2,1)}, u32[]{:S(2)}) copy-start(bf16[128,512]{1,0:T(8,128)(2,1)} %pw_ref.1) | copy-start | bytes 393220
  2.6 0.8 %copy-start.2 = (bf16[128,128]{1,0:T(8,128)(2,1)S(1)}, bf16[128,128]{1,0:T(8,128)(2,1)}, u32[]{:S(2)}) copy-start(bf16[128,128]{1,0:T(8,128)(2,1)} %gw_ref.1) | copy-start | bytes 98308
  3.4 0.8 %copy-start.3 = (bf16[128,128]{1,0:T(8,128)(2,1)S(1)}, bf16[128,128]{1,0:T(8,128)(2,1)}, u32[]{:S(2)}) copy-start(bf16[128,128]{1,0:T(8,128)(2,1)} %ow_ref.1) | copy-start | bytes 98308

commit v2 on v1

v2 whole, which is shorter than its diff:
```python
import jax
import jax.numpy as jnp
from jax import lax
from jax.experimental import pallas as pl
from jax.experimental.pallas import tpu as pltpu
from jax.sharding import PartitionSpec as P

MESH = pl.DeviceIdType.MESH
BF16 = jnp.bfloat16
F32 = jnp.float32
EPS = 1e-05

NX, NY, NZ = 4, 4, 8
CHIPS = NX * NY * NZ


def place():
    row, col = lax.axis_index("row"), lax.axis_index("col")
    core = lax.rem(row, 2)
    y = lax.rem(lax.div(row, 2), NY)
    x = lax.div(col, NZ) * 2 + lax.div(row, 2 * NY)
    return x, y, lax.rem(col, NZ), core


def device(x, y, z, core):
    return lax.rem(x, 2) * 8 + y * 2 + core, lax.div(x, 2) * NZ + z


def transpose_blocks(v, lane):
    low, even = lane < 64, lax.rem(lax.div(lane, 32), 2) == 0
    u0 = jnp.where(low, v[0], pltpu.roll(v[2], 64, 1))
    u2 = jnp.where(low, pltpu.roll(v[0], 64, 1), v[2])
    u1 = jnp.where(low, v[1], pltpu.roll(v[3], 64, 1))
    u3 = jnp.where(low, pltpu.roll(v[1], 64, 1), v[3])
    return (
        jnp.where(even, u0, pltpu.roll(u1, 32, 1)),
        jnp.where(even, pltpu.roll(u0, 96, 1), u1),
        jnp.where(even, u2, pltpu.roll(u3, 32, 1)),
        jnp.where(even, pltpu.roll(u2, 96, 1), u3),
    )


def column(vec, width):
    return jnp.transpose(jnp.broadcast_to(vec, (width, vec.shape[1])))


ORDER = (4, 3, 5, 2, 6, 1, 7, 0)
WAVES = ((3, 5), (4, 0), (2, 6), (1, 7))


def kernel(
    x_hbm, ng_hbm, nb_hbm, pw_hbm, pb_hbm, gw_hbm, gb_hbm, mg_hbm, mb_hbm, ow_hbm, ob_hbm,
    out_ref,
    x_ref, ng_ref, nb_ref, pw_ref, pb_ref, gw_ref, gb_ref, mg_ref, mb_ref, ow_ref, ob_ref, load_sem,
    xn, wt, pbt, grp_l, grp_r, send_l, send_r, recv_l, recv_r, left, left_t, right, part, part_in,
    total, back, back_in, mixed, gate, mgt, mbt,
    send_sem, left_sem, right_sem, part_send, part_recv, back_send, back_recv,
):
    loads = [
        pltpu.make_async_copy(src, dst, load_sem.at[i])
        for i, (src, dst) in enumerate(
            (
                (x_hbm, x_ref), (ng_hbm, ng_ref), (nb_hbm, nb_ref), (pw_hbm, pw_ref),
                (pb_hbm, pb_ref), (gw_hbm, gw_ref), (gb_hbm, gb_ref), (mg_hbm, mg_ref),
                (mb_hbm, mb_ref), (ow_hbm, ow_ref), (ob_hbm, ob_ref),
            )
        )
    ]
    for load in loads:
        load.start()
    x, y, z, core = place()
    rows, cols = device(x, y, z, core)
    slot = lax.div(rows, 2) * 16 + cols
    chan = z * 16 + x * NY + y
    partner = device(x, y, z, 1 - core)
    zs = [lax.rem(z + d, NZ) for d in range(NZ)]

    def each_plane(act):
        def step(i, carry):
            tx, ty = lax.rem(x + lax.div(i, 4) + 2, NX), lax.rem(y + lax.rem(i, 4) + 2, NY)
            act(i, tx, ty)
            return carry

        lax.fori_loop(0, 16, step, 0)

    barrier = pltpu.get_barrier_semaphore()

    def greet(i, tx, ty):
        for d in ORDER:

            def signal(tz=zs[d]):
                pl.semaphore_signal(
                    barrier, inc=1, device_id=device(tx, ty, tz, core), device_id_type=MESH
                )

            if d == 0:
                pl.when(i != 10)(signal)
            else:
                signal()

    each_plane(greet)
    pl.semaphore_signal(barrier, inc=1, device_id=partner, device_id_type=MESH)

    for load in loads:
        load.wait()
    for t in range(8):
        chunk = pl.ds(t * 128, 128)
        v = x_ref[chunk, :].astype(F32)
        center = v - jnp.mean(v, axis=1, keepdims=True)
        spread = jnp.mean(center * center, axis=1, keepdims=True)
        xn[chunk, :] = (center * lax.rsqrt(spread + EPS) * ng_ref[...] + nb_ref[...]).astype(BF16)
    for b in range(4):
        weight = jnp.transpose(pw_ref[:, b * 128 : (b + 1) * 128])
        bias = column(pb_ref[:, b * 128 : (b + 1) * 128], 128)
        for h in range(2):
            wt[pl.ds(h * 256 + b * 64, 64), :] = weight[h * 64 : (h + 1) * 64]
            pbt[pl.ds(h * 256 + b * 64, 64), :] = bias[h * 64 : (h + 1) * 64]

    def project(h):
        for pair in range(4):
            proj = lax.dot_general(
                wt[pl.ds(h * 256, 256), :],
                xn[pl.ds(pair * 256, 256), :],
                (((1,), (1,)), ((), ())),
                preferred_element_type=F32,
            )
            for s in range(2):
                t = pair * 2 + s
                p = [
                    proj[b * 64 : (b + 1) * 64, s * 128 : (s + 1) * 128]
                    + pbt[pl.ds(h * 256 + b * 64, 64), :]
                    for b in range(4)
                ]
                grp_l[pl.ds(t, 64, stride=8), :] = jax.nn.sigmoid(p[0]) * p[1]
                grp_r[pl.ds(t, 64, stride=8), :] = jax.nn.sigmoid(p[2]) * p[3]
        send_l[pl.ds(h * 64, 64)] = grp_l[...].reshape(64, 8, 128).astype(BF16)
        send_r[pl.ds(h * 64, 64)] = grp_r[...].reshape(64, 8, 128).astype(BF16)

    def spread_out(dzs, source, store, sem):
        def push(i, tx, ty):
            for d in dzs:
                target = zs[d] * 16 + tx * NY + ty

                def go(tz=zs[d], target=target):
                    pltpu.make_async_remote_copy(
                        src_ref=source.at[target],
                        dst_ref=store.at[slot],
                        send_sem=send_sem,
                        recv_sem=sem,
                        device_id=device(tx, ty, tz, core),
                        device_id_type=MESH,
                    ).start()

                if d == 0:
                    pl.when(i != 10)(go)
                else:
                    go()

        each_plane(push)

    project(0)
    project(1)

    pl.semaphore_wait(barrier, CHIPS)

    spread_out(ORDER, send_l, recv_l, left_sem)
    for w, wave in enumerate(WAVES):
        spread_out(wave, send_r, recv_r, right_sem.at[w])
    recv_l[slot] = send_l[chan]
    recv_r[slot] = send_r[chan]

    for t in range(8):
        chunk = pl.ds(t * 128, 128)
        gate[chunk, :] = jax.nn.sigmoid(
            jnp.dot(xn[chunk, :], gw_ref[...], preferred_element_type=F32) + gb_ref[...]
        )
    mgt[...] = column(mg_ref[...], 128)
    mbt[...] = column(mb_ref[...], 128)

    landed = recv_l.at[pl.ds(0, CHIPS - 1)]
    pltpu.make_async_copy(landed, landed, left_sem).wait()

    lane = lax.broadcasted_iota(jnp.int32, (16, 128), 1)

    def regroup(source, cs, store, first):
        for p in range(4):
            tiles = [
                jnp.concatenate(
                    [source[(2 * p + q) * 16 + c].astype(F32) for q in range(2)], axis=0
                )
                for c in cs
            ]
            for k4, tile in enumerate(transpose_blocks(tiles, lane)):
                store[pl.ds(k4 * 64 + p * 16, 16), pl.ds(first, 128)] = tile.astype(BF16)

    for g in range(4):
        regroup(recv_l, [(g % 2) * 8 + 2 * m + g // 2 for m in range(4)], left, g * 128)
    for g in range(4):
        for h in range(2):
            block = left[pl.ds(h * 128, 128), pl.ds(g * 128, 128)]
            left_t[pl.ds(g * 128, 128), pl.ds(h * 128, 128)] = jnp.transpose(block)

    lane8 = lax.broadcasted_iota(jnp.int32, (8, 128), 1)

    def product(which, w):
        start = pl.multiple_of(which * 256, 256)
        return jnp.dot(left_t[pl.ds(start, 256), :], right[w], preferred_element_type=F32)

    def multiply(w):
        wave = WAVES[w]
        arrived = recv_r.at[pl.ds(0, 31 if 0 in wave else 32)]
        pltpu.make_async_copy(arrived, arrived, right_sem.at[w]).wait()
        cs = [(m % 2) * 8 + zs[(8 - wave[m // 2]) % 8] for m in range(4)]
        regroup(recv_r, cs, right.at[w], 0)
        part[w] = product(1 - core, w)
        swap = pltpu.make_async_remote_copy(
            src_ref=part.at[w],
            dst_ref=part_in.at[w],
            send_sem=part_send.at[w],
            recv_sem=part_recv.at[w],
            device_id=partner,
            device_id_type=MESH,
        )
        swap.start()
        total[w] = product(core, w)
        return swap

    def give(w, swap):
        swap.wait_recv()
        places = []
        for i in range(8):
            lo, ty = lax.rem(x + 1 + i // 4, 2), lax.rem(y + 2 + i, NY)
            b = lo * NY + ty
            tiles = []
            for q in range(4):
                here = pl.ds(pl.multiple_of(b * 32 + q * 8, 8), 8)
                tiles.append(total[w, here, :] + part_in[w, here, :])
            for m, tile in enumerate(transpose_blocks(tiles, lane8)):
                tx, d = (m % 2) * 2 + lo, (8 - WAVES[w][m // 2]) % 8
                target = zs[d] * 16 + tx * NY + ty
                back[target] = tile.astype(BF16)
                places.append(((b * 2 + core, (m % 2) * NZ + zs[d]), target, d))
        for peer, target, d in places:

            def go(peer=peer, target=target):
                pltpu.make_async_remote_copy(
                    src_ref=back.at[target],
                    dst_ref=back_in.at[chan],
                    send_sem=back_send,
                    recv_sem=back_recv,
                    device_id=peer,
                    device_id_type=MESH,
                ).start()

            if d == 0:
                pl.when(target != chan)(go)
            else:
                go()

    swaps = [multiply(0), multiply(1)]
    give(0, swaps[0])
    swaps.append(multiply(2))
    give(1, swaps[1])
    swaps.append(multiply(3))
    give(2, swaps[2])
    give(3, swaps[3])
    back_in[chan] = back[chan]

    came = back_in.at[pl.ds(0, CHIPS - 1)]
    pltpu.make_async_copy(came, came, back_recv).wait()

    values = back_in[...].astype(F32)
    center = values - jnp.mean(values, axis=0, keepdims=True)
    spread = jnp.mean(center * center, axis=0, keepdims=True)
    mixed[...] = (center * lax.rsqrt(spread + EPS)).reshape(1024, 128)
    for t in range(8):
        norm = mixed[pl.ds(t, 128, stride=8), :] * mgt[...] + mbt[...]
        res = lax.dot_general(
            norm.astype(BF16),
            ow_ref[...],
            (((0,), (0,)), ((), ())),
            preferred_element_type=F32,
        ) + ob_ref[...]
        for q in range(4):
            where = pl.ds(q * 256 + t * 32, 32)
            out_ref[where, :] = (gate[where, :] * res[q * 32 : (q + 1) * 32]).astype(BF16)

    for sent in (send_l, send_r):
        gone = sent.at[pl.ds(0, CHIPS - 1)]
        pltpu.make_async_copy(gone, gone, send_sem).wait()
    for swap in swaps:
        swap.wait_send()
    gone = back.at[pl.ds(0, CHIPS - 1)]
    pltpu.make_async_copy(gone, gone, back_send).wait()


def per_device(
    pair_act, norm_gain, norm_bias, proj_weight, proj_bias, gate_weight, gate_bias, mid_gain,
    mid_bias, out_weight, out_bias,
):
    dma = pltpu.SemaphoreType.DMA
    vmem = pltpu.VMEM
    out = pl.pallas_call(
        kernel,
        out_shape=jax.ShapeDtypeStruct((1024, 128), BF16),
        in_specs=[pl.BlockSpec(memory_space=pl.ANY)] * 11,
        out_specs=pl.BlockSpec(memory_space=vmem),
        scratch_shapes=[
            vmem((1024, 128), BF16),
            vmem((1, 128), F32),
            vmem((1, 128), F32),
            vmem((128, 512), BF16),
            vmem((1, 512), F32),
            vmem((128, 128), BF16),
            vmem((1, 128), F32),
            vmem((1, 128), F32),
            vmem((1, 128), F32),
            vmem((128, 128), BF16),
            vmem((1, 128), F32),
            dma((11,)),
            vmem((1024, 128), BF16),
            vmem((512, 128), BF16),
            vmem((512, 128), F32),
            vmem((512, 128), F32),
            vmem((512, 128), F32),
            vmem((CHIPS, 8, 128), BF16),
            vmem((CHIPS, 8, 128), BF16),
            vmem((CHIPS, 8, 128), BF16),
            vmem((CHIPS, 8, 128), BF16),
            vmem((256, 512), BF16),
            vmem((512, 256), BF16),
            vmem((4, 256, 128), BF16),
            vmem((4, 256, 128), F32),
            vmem((4, 256, 128), F32),
            vmem((4, 256, 128), F32),
            vmem((CHIPS, 8, 128), BF16),
            vmem((CHIPS, 8, 128), BF16),
            vmem((1024, 128), F32),
            vmem((1024, 128), F32),
            vmem((128, 128), F32),
            vmem((128, 128), F32),
            dma, dma, dma((4,)), dma((4,)), dma((4,)), dma, dma,
        ],
        compiler_params=pltpu.CompilerParams(
            collective_id=0, has_side_effects=True, vmem_limit_bytes=56 << 20
        ),
        cost_estimate=pl.CostEstimate(
            flops=500_000_000, bytes_accessed=2_000_000, transcendentals=1_000_000
        ),
        name="triangle",
    )(
        pair_act.reshape(1024, 128),
        norm_gain.reshape(1, -1),
        norm_bias.reshape(1, -1),
        proj_weight,
        proj_bias.reshape(1, -1),
        gate_weight,
        gate_bias.reshape(1, -1),
        mid_gain.reshape(1, -1),
        mid_bias.reshape(1, -1),
        out_weight,
        out_bias.reshape(1, -1),
    )
    return out.reshape(32, 32, 128)


def solution(mesh):
    placed = (P("row", "col", None),) + (P(),) * 10
    return jax.shard_map(
        per_device, mesh=mesh, in_specs=placed, out_specs=P("row", "col", None), check_vma=False
    )
```

time: 48.8 us -> 42.8 us (0.88)
  local copies, waits for them, and re-layouts: 4.78 us -> 1.67 us
  Pallas kernels: 43.7 us -> 41 us
    unnamed x23 -> x1, local copies, waits for them, and re-layouts: 4.78 us -> 1.67 us
    pallas_call x1, Pallas kernels: 43.7 us -> 41 us  [per_device(): pl.pallas_call(kernel, out_shape=jax.ShapeDtypeStruct((1024, 128), BF16),...]
where the time goes in v2:
time: 42.8 us; the launch traced here: 42.7 us
  Pallas kernels  41 us (96%)
  local copies, waits for them, and re-layouts  1.67 us (4%)
    pallas_call x1, Pallas kernels, per_device(): pl.pallas_call(kernel, out_shape=jax.ShapeDtypeStruct((1024, 128), BF16),...  41 us
    unnamed x1, local copies, waits for them, and re-layouts  1.67 us

profile of v2, /device:TPU:1, one launch (start us, length us, event | category | flops | bytes accessed | tf_op | source)
XLA Modules:
  0.0 42.7 jit_solution(12461270037638043339)
XLA Ops:
  0.0 41.0 %triangle.1 = bf16[1024,128]{1,0:T(8,128)(2,1)} custom-call(bf16[1024,128]{1,0:T(8,128)(2,1)} %bitcast.10, f32[1,128]{1,0:T(1,128)} %bitcast.12, f32[1,128]{1,0:T(1,128)} %bitcast.13, bf16[128,512]{1,0:T(8,128)(2,1)} %pw_hbm.1, f32[1,512]{1,0:T(1,128)} %bitcast.11, bf16[128,128]{1,0:T(8,128)(2,1)} %gw_hbm.1, f32[1,128]{1,0:T(1,128)} %bitcast.14, ...), custom_call_target="tpu_custom_call" | custom-call | flops 500000000 | bytes 2000000 | tf_op jit(solution)/shard_map/triangle/pallas_call | solution.py:303
  41.0 1.7 %copy.13 = bf16[32,32,128]{2,1,0:T(8,128)(2,1)} copy(bf16[32,32,128]{2,1,0:T(8,128)(2,1)} %bitcast.9) | data formatting | bytes 524288

commit v3 on v2

v3 whole, which is shorter than its diff:
```python
import jax
import jax.numpy as jnp
from jax import lax
from jax.experimental import pallas as pl
from jax.experimental.pallas import tpu as pltpu
from jax.sharding import PartitionSpec as P

MESH = pl.DeviceIdType.MESH
BF16 = jnp.bfloat16
F32 = jnp.float32
EPS = 1e-05

NX, NY, NZ = 4, 4, 8
CHIPS = NX * NY * NZ


def place():
    row, col = lax.axis_index("row"), lax.axis_index("col")
    core = lax.rem(row, 2)
    y = lax.rem(lax.div(row, 2), NY)
    x = lax.div(col, NZ) * 2 + lax.div(row, 2 * NY)
    return x, y, lax.rem(col, NZ), core


def device(x, y, z, core):
    return lax.rem(x, 2) * 8 + y * 2 + core, lax.div(x, 2) * NZ + z


def transpose_blocks(v, lane):
    low, even = lane < 64, lax.rem(lax.div(lane, 32), 2) == 0
    u0 = jnp.where(low, v[0], pltpu.roll(v[2], 64, 1))
    u2 = jnp.where(low, pltpu.roll(v[0], 64, 1), v[2])
    u1 = jnp.where(low, v[1], pltpu.roll(v[3], 64, 1))
    u3 = jnp.where(low, pltpu.roll(v[1], 64, 1), v[3])
    return (
        jnp.where(even, u0, pltpu.roll(u1, 32, 1)),
        jnp.where(even, pltpu.roll(u0, 96, 1), u1),
        jnp.where(even, u2, pltpu.roll(u3, 32, 1)),
        jnp.where(even, pltpu.roll(u2, 96, 1), u3),
    )


def column(vec, width):
    return jnp.transpose(jnp.broadcast_to(vec, (width, vec.shape[1])))


WAVES = (
    ((1, 4), (1, 3), (1, 5), (0, 4)),
    ((1, 2), (1, 6), (0, 3), (0, 5)),
    ((1, 1), (1, 7), (0, 2), (0, 6)),
    ((1, 0), (0, 1), (0, 7), (0, 0)),
)
TO_CORE = (0, 1, 1, 0)
ROWS = (1, 0, 9, 8, 3, 2, 11, 10, 5, 4, 13, 12, 7, 6, 15, 14)


def kernel(
    x_hbm, ng_hbm, nb_hbm, pw_hbm, pb_hbm, gw_hbm, gb_hbm, mg_hbm, mb_hbm, ow_hbm, ob_hbm,
    out_hbm,
    x_ref, ng_ref, nb_ref, pw_ref, pb_ref, gw_ref, gb_ref, mg_ref, mb_ref, ow_ref, ob_ref, load_sem,
    xn, wt, pbt, grp_l, grp_r, send_l, send_r, recv_l, mate_l, recv_r, left, left_t, right, total,
    back, back_in, mixed, gate, mgt, mbt, result,
    send_sem, left_sem, right_sem, mate_send, mate_recv, back_send, back_recv, out_sem, mate_sem,
):
    loads = [
        pltpu.make_async_copy(src, dst, load_sem.at[i])
        for i, (src, dst) in enumerate(
            (
                (x_hbm, x_ref), (ng_hbm, ng_ref), (nb_hbm, nb_ref), (pw_hbm, pw_ref),
                (pb_hbm, pb_ref), (gw_hbm, gw_ref), (gb_hbm, gb_ref), (mg_hbm, mg_ref),
                (mb_hbm, mb_ref), (ow_hbm, ow_ref), (ob_hbm, ob_ref),
            )
        )
    ]
    for load in loads:
        load.start()
    x, y, z, core = place()
    rows, cols = device(x, y, z, core)
    slot = lax.div(rows, 2) * 16 + cols
    chan = z * 16 + x * NY + y
    partner = device(x, y, z, 1 - core)
    x_lo, x_hi = lax.rem(x, 2), lax.div(x, 2)

    def send_waves(act):
        for w, wave in enumerate(WAVES):
            chips = []
            for hi, d in wave:
                txh, tz = lax.rem(x_hi + hi, 2), lax.rem(z + d, NZ)
                chips.append(((hi, d) == (0, 0), tz * 16 + txh * 8, txh * NZ + tz))

            def step(i, carry, w=w, chips=chips):
                base = lax.rem(x_lo + 1 + lax.div(i, 4), 2) * NY + lax.rem(y + 2 + i, NY)
                for mine, to_chan, to_col in chips:
                    act(w, jnp.logical_and(i == 6, mine) if mine else None, base, to_chan, to_col)
                return carry

            lax.fori_loop(0, 8, step, 0)

    barrier = pltpu.get_barrier_semaphore()

    def greet(w, mine, base, to_chan, to_col):
        def signal():
            pl.semaphore_signal(
                barrier, inc=1, device_id=(base * 2 + core, to_col), device_id_type=MESH
            )

        if mine is None:
            signal()
        else:
            pl.when(jnp.logical_not(mine))(signal)

    send_waves(greet)
    pl.semaphore_signal(barrier, inc=1, device_id=partner, device_id_type=MESH)

    for load in loads:
        load.wait()
    for t in range(8):
        chunk = pl.ds(t * 128, 128)
        v = x_ref[chunk, :].astype(F32)
        center = v - jnp.mean(v, axis=1, keepdims=True)
        spread = jnp.mean(center * center, axis=1, keepdims=True)
        xn[chunk, :] = (center * lax.rsqrt(spread + EPS) * ng_ref[...] + nb_ref[...]).astype(BF16)
    for b in range(4):
        weight = jnp.transpose(pw_ref[:, b * 128 : (b + 1) * 128])
        bias = column(pb_ref[:, b * 128 : (b + 1) * 128], 128)
        for h in range(2):
            wt[pl.ds(h * 256 + b * 64, 64), :] = weight[h * 64 : (h + 1) * 64]
            pbt[pl.ds(h * 256 + b * 64, 64), :] = bias[h * 64 : (h + 1) * 64]

    def project(h):
        for pair in range(4):
            proj = lax.dot_general(
                wt[pl.ds(h * 256, 256), :],
                xn[pl.ds(pair * 256, 256), :],
                (((1,), (1,)), ((), ())),
                preferred_element_type=F32,
            )
            for s in range(2):
                t = pair * 2 + s
                p = [
                    proj[b * 64 : (b + 1) * 64, s * 128 : (s + 1) * 128]
                    + pbt[pl.ds(h * 256 + b * 64, 64), :]
                    for b in range(4)
                ]
                grp_l[pl.ds(t, 64, stride=8), :] = jax.nn.sigmoid(p[0]) * p[1]
                grp_r[pl.ds(t, 64, stride=8), :] = jax.nn.sigmoid(p[2]) * p[3]
        send_l[pl.ds(h * 64, 64)] = grp_l[...].reshape(64, 8, 128).astype(BF16)
        send_r[pl.ds(h * 64, 64)] = grp_r[...].reshape(64, 8, 128).astype(BF16)

    project(0)
    project(1)

    pl.semaphore_wait(barrier, CHIPS)
    pl.semaphore_signal(mate_sem, inc=1, device_id=partner, device_id_type=MESH)

    def push_left(w, mine, base, to_chan, to_col):
        def go():
            pltpu.make_async_remote_copy(
                src_ref=send_l.at[to_chan + base],
                dst_ref=recv_l.at[slot],
                send_sem=send_sem,
                recv_sem=left_sem,
                device_id=(base * 2 + core, to_col),
                device_id_type=MESH,
            ).start()

        if mine is None:
            go()
        else:
            pl.when(jnp.logical_not(mine))(go)

    def push_right(w, mine, base, to_chan, to_col):
        def go():
            pltpu.make_async_remote_copy(
                src_ref=send_r.at[to_chan + base],
                dst_ref=recv_r.at[core, slot],
                send_sem=send_sem,
                recv_sem=right_sem.at[w // 2],
                device_id=(base * 2 + TO_CORE[w], to_col),
                device_id_type=MESH,
            ).start()

        if mine is None:
            go()
        else:
            pl.when(jnp.logical_not(jnp.logical_and(mine, core == TO_CORE[w])))(go)

    send_waves(push_left)
    pl.semaphore_wait(mate_sem, 1)
    send_waves(push_right)
    recv_l[slot] = send_l[chan]

    @pl.when(core == TO_CORE[3])
    def _():
        pltpu.make_async_copy(send_r.at[chan], recv_r.at[core, slot], right_sem.at[1]).start()

    for t in range(8):
        chunk = pl.ds(t * 128, 128)
        gate[chunk, :] = jax.nn.sigmoid(
            jnp.dot(xn[chunk, :], gw_ref[...], preferred_element_type=F32) + gb_ref[...]
        )
    mgt[...] = column(mg_ref[...], 128)
    mbt[...] = column(mb_ref[...], 128)

    landed = recv_l.at[pl.ds(0, CHIPS - 1)]
    pltpu.make_async_copy(landed, landed, left_sem).wait()

    swap = pltpu.make_async_remote_copy(
        src_ref=recv_l,
        dst_ref=mate_l,
        send_sem=mate_send,
        recv_sem=mate_recv,
        device_id=partner,
        device_id_type=MESH,
    )
    swap.start()

    lane = lax.broadcasted_iota(jnp.int32, (16, 128), 1)

    def regroup(source, cs, store, row, first):
        for p in range(4):
            tiles = [
                jnp.concatenate(
                    [source[(2 * p + q) * 16 + c].astype(F32) for q in range(2)], axis=0
                )
                for c in cs
            ]
            for k4, tile in enumerate(transpose_blocks(tiles, lane)):
                store[pl.ds(row + k4 * 64 + p * 16, 16), pl.ds(first, 128)] = tile.astype(BF16)

    for half, source in enumerate((recv_l, mate_l)):
        if half == 1:
            swap.wait_recv()
        for g in range(4):
            regroup(source, [4 * g + m for m in range(4)], left, half * 256, g * 128)
        for g in range(4):
            for h in range(2):
                block = left[pl.ds(half * 256 + h * 128, 128), pl.ds(g * 128, 128)]
                left_t[pl.ds(g * 128, 128), pl.ds(half * 256 + h * 128, 128)] = jnp.transpose(block)

    lane8 = lax.broadcasted_iota(jnp.int32, (8, 128), 1)

    def multiply(j):
        arrived = recv_r.at[0, pl.ds(0, 64)]
        pltpu.make_async_copy(arrived, arrived, right_sem.at[j]).wait()
        for half, source in enumerate((recv_r.at[core], recv_r.at[1 - core])):
            regroup(source, came_from[j], right.at[j], half * 256, 0)
        total[j] = jnp.dot(left_t[...], right[j], preferred_element_type=F32)

    def give(j):
        places = []
        for i in range(16):
            row = ROWS[i]
            tiles = []
            for q in range(4):
                here = pl.ds(row * 32 + q * 8, 8)
                tiles.append(total[j, here, :])
            for m, tile in enumerate(transpose_blocks(tiles, lane8)):
                place_in = j * 64 + i * 4 + m
                back[place_in] = tile.astype(BF16)
                places.append((row, came_from[j][m], place_in, j == 1 and m == 3))
        for row, col, place_in, maybe_here in places:

            def go(row=row, col=col, place_in=place_in):
                pltpu.make_async_remote_copy(
                    src_ref=back.at[place_in],
                    dst_ref=back_in.at[chan],
                    send_sem=back_send,
                    recv_sem=back_recv,
                    device_id=(row, col),
                    device_id_type=MESH,
                ).start()

            if maybe_here:
                here = jnp.logical_and(row == rows, col == cols)
                pl.when(jnp.logical_not(here))(go)

                @pl.when(here)
                def _(place_in=place_in):
                    pltpu.make_async_copy(back.at[place_in], back_in.at[chan], back_recv).start()

            else:
                go()

    came_from = []
    for w0, w1 in ((0, 1), (3, 2)):
        cols_of = []
        for (hi0, d0), (hi1, d1) in zip(WAVES[w0], WAVES[w1]):
            hi, d = jnp.where(core == 0, hi0, hi1), jnp.where(core == 0, d0, d1)
            cols_of.append(lax.rem(x_hi + hi, 2) * NZ + lax.rem(z + NZ - d, NZ))
        came_from.append(cols_of)
    multiply(0)
    give(0)
    multiply(1)
    give(1)

    pltpu.make_async_copy(back_in, back_in, back_recv).wait()

    values = back_in[...].astype(F32)
    center = values - jnp.mean(values, axis=0, keepdims=True)
    spread = jnp.mean(center * center, axis=0, keepdims=True)
    mixed[...] = (center * lax.rsqrt(spread + EPS)).reshape(1024, 128)
    writes = []
    for t in range(8):
        norm = mixed[pl.ds(t, 128, stride=8), :] * mgt[...] + mbt[...]
        res = lax.dot_general(
            norm.astype(BF16),
            ow_ref[...],
            (((0,), (0,)), ((), ())),
            preferred_element_type=F32,
        ) + ob_ref[...]
        for q in range(4):
            where = pl.ds(q * 256 + t * 32, 32)
            result[q, t] = (gate[where, :] * res[q * 32 : (q + 1) * 32]).astype(BF16)
        if t % 2:
            pair = pl.ds(t - 1, 2)
            write = pltpu.make_async_copy(
                result.at[:, pair], out_hbm.at[:, pair], out_sem.at[t // 2]
            )
            write.start()
            writes.append(write)

    for write in writes:
        write.wait()
    swap.wait_send()
    for gone, sem in ((send_l, send_sem), (send_r, send_sem), (back, back_send)):
        most = gone.at[pl.ds(0, CHIPS - 1)]
        pltpu.make_async_copy(most, most, sem).wait()

    @pl.when(core != TO_CORE[3])
    def _():
        for gone, sem in ((send_r, send_sem), (back, back_send)):
            last = gone.at[pl.ds(0, 1)]
            pltpu.make_async_copy(last, last, sem).wait()


def per_device(
    pair_act, norm_gain, norm_bias, proj_weight, proj_bias, gate_weight, gate_bias, mid_gain,
    mid_bias, out_weight, out_bias,
):
    dma = pltpu.SemaphoreType.DMA
    vmem = pltpu.VMEM
    out = pl.pallas_call(
        kernel,
        out_shape=jax.ShapeDtypeStruct((4, 8, 32, 128), BF16),
        in_specs=[pl.BlockSpec(memory_space=pl.ANY)] * 11,
        out_specs=pl.BlockSpec(memory_space=pl.ANY),
        scratch_shapes=[
            vmem((1024, 128), BF16),
            vmem((1, 128), F32),
            vmem((1, 128), F32),
            vmem((128, 512), BF16),
            vmem((1, 512), F32),
            vmem((128, 128), BF16),
            vmem((1, 128), F32),
            vmem((1, 128), F32),
            vmem((1, 128), F32),
            vmem((128, 128), BF16),
            vmem((1, 128), F32),
            dma((11,)),
            vmem((1024, 128), BF16),
            vmem((512, 128), BF16),
            vmem((512, 128), F32),
            vmem((512, 128), F32),
            vmem((512, 128), F32),
            vmem((CHIPS, 8, 128), BF16),
            vmem((CHIPS, 8, 128), BF16),
            vmem((CHIPS, 8, 128), BF16),
            vmem((CHIPS, 8, 128), BF16),
            vmem((2, CHIPS, 8, 128), BF16),
            vmem((512, 512), BF16),
            vmem((512, 512), BF16),
            vmem((2, 512, 128), BF16),
            vmem((2, 512, 128), F32),
            vmem((CHIPS, 8, 128), BF16),
            vmem((CHIPS, 8, 128), BF16),
            vmem((1024, 128), F32),
            vmem((1024, 128), F32),
            vmem((128, 128), F32),
            vmem((128, 128), F32),
            vmem((4, 8, 32, 128), BF16),
            dma, dma, dma((2,)), dma, dma, dma, dma, dma((4,)), pltpu.SemaphoreType.REGULAR,
        ],
        compiler_params=pltpu.CompilerParams(
            collective_id=0, has_side_effects=True, vmem_limit_bytes=56 << 20
        ),
        cost_estimate=pl.CostEstimate(
            flops=500_000_000, bytes_accessed=2_000_000, transcendentals=1_000_000
        ),
        name="triangle",
    )(
        pair_act.reshape(1024, 128),
        norm_gain.reshape(1, -1),
        norm_bias.reshape(1, -1),
        proj_weight,
        proj_bias.reshape(1, -1),
        gate_weight,
        gate_bias.reshape(1, -1),
        mid_gain.reshape(1, -1),
        mid_bias.reshape(1, -1),
        out_weight,
        out_bias.reshape(1, -1),
    )
    return out.reshape(32, 32, 128)


def solution(mesh):
    placed = (P("row", "col", None),) + (P(),) * 10
    return jax.shard_map(
        per_device, mesh=mesh, in_specs=placed, out_specs=P("row", "col", None), check_vma=False
    )
```

time: 42.8 us -> 40.3 us (0.942)
  Pallas kernels: 41 us -> 38.5 us
    pallas_call x1, Pallas kernels: 41 us -> 38.5 us  [per_device(): pl.pallas_call(kernel, out_shape=jax.ShapeDtypeStruct((4, 8, 32, 128), BF...]
where the time goes in v3:
time: 40.3 us; the launch traced here: 40.2 us
  Pallas kernels  38.5 us (96%)
  local copies, waits for them, and re-layouts  1.67 us (4%)
    pallas_call x1, Pallas kernels, per_device(): pl.pallas_call(kernel, out_shape=jax.ShapeDtypeStruct((4, 8, 32, 128), BF...  38.5 us
    unnamed x1, local copies, waits for them, and re-layouts  1.67 us

profile of v3, /device:TPU:1, one launch (start us, length us, event | category | flops | bytes accessed | tf_op | source)
XLA Modules:
  0.0 40.2 jit_solution(6815862140867122466)
XLA Ops:
  0.0 38.5 %triangle.1 = bf16[4,8,32,128]{3,2,1,0:T(8,128)(2,1)} custom-call(bf16[1024,128]{1,0:T(8,128)(2,1)} %bitcast.10, f32[1,128]{1,0:T(1,128)} %bitcast.12, f32[1,128]{1,0:T(1,128)} %bitcast.13, bf16[128,512]{1,0:T(8,128)(2,1)} %pw_hbm.1, f32[1,512]{1,0:T(1,128)} %bitcast.11, bf16[128,128]{1,0:T(8,128)(2,1)} %gw_hbm.1, f32[1,128]{1,0:T(1,128)} %bitcast.14, ...), custom_call_target="tpu_custom_call" | custom-call | flops 500000000 | bytes 2000000 | tf_op jit(solution)/shard_map/triangle/pallas_call | solution.py:343
  38.5 1.7 %copy.13 = bf16[32,32,128]{2,1,0:T(8,128)(2,1)} copy(bf16[32,32,128]{2,1,0:T(8,128)(2,1)} %bitcast.9) | data formatting | bytes 524288

commit v4 on v3

--- a/solution.py
+++ b/solution.py
@@ -55,11 +55,11 @@
 
 
 def kernel(
-    x_hbm, ng_hbm, nb_hbm, pw_hbm, pb_hbm, gw_hbm, gb_hbm, mg_hbm, mb_hbm, ow_hbm, ob_hbm,
-    out_hbm,
-    x_ref, ng_ref, nb_ref, pw_ref, pb_ref, gw_ref, gb_ref, mg_ref, mb_ref, ow_ref, ob_ref, load_sem,
+    x_hbm, ng_hbm, nb_hbm, pw_hbm, pb_hbm, gw_hbm, gb_hbm,
+    back_in, gate_hbm,
+    x_ref, ng_ref, nb_ref, pw_ref, pb_ref, gw_ref, gb_ref, load_sem,
     xn, wt, pbt, grp_l, grp_r, send_l, send_r, recv_l, mate_l, recv_r, left, left_t, right, total,
-    back, back_in, mixed, gate, mgt, mbt, result,
+    back, gate,
     send_sem, left_sem, right_sem, mate_send, mate_recv, back_send, back_recv, out_sem, mate_sem,
 ):
     loads = [
@@ -67,8 +67,7 @@
         for i, (src, dst) in enumerate(
             (
                 (x_hbm, x_ref), (ng_hbm, ng_ref), (nb_hbm, nb_ref), (pw_hbm, pw_ref),
-                (pb_hbm, pb_ref), (gw_hbm, gw_ref), (gb_hbm, gb_ref), (mg_hbm, mg_ref),
-                (mb_hbm, mb_ref), (ow_hbm, ow_ref), (ob_hbm, ob_ref),
+                (pb_hbm, pb_ref), (gw_hbm, gw_ref), (gb_hbm, gb_ref),
             )
         )
     ]
@@ -199,8 +198,8 @@
         gate[chunk, :] = jax.nn.sigmoid(
             jnp.dot(xn[chunk, :], gw_ref[...], preferred_element_type=F32) + gb_ref[...]
         )
-    mgt[...] = column(mg_ref[...], 128)
-    mbt[...] = column(mb_ref[...], 128)
+    keep = pltpu.make_async_copy(gate, gate_hbm, out_sem)
+    keep.start()
 
     landed = recv_l.at[pl.ds(0, CHIPS - 1)]
     pltpu.make_async_copy(landed, landed, left_sem).wait()
@@ -296,10 +295,52 @@
 
     pltpu.make_async_copy(back_in, back_in, back_recv).wait()
 
+    keep.wait()
+    swap.wait_send()
+    for gone, sem in ((send_l, send_sem), (send_r, send_sem), (back, back_send)):
+        most = gone.at[pl.ds(0, CHIPS - 1)]
+        pltpu.make_async_copy(most, most, sem).wait()
+
+    @pl.when(core != TO_CORE[3])
+    def _():
+        for gone, sem in ((send_r, send_sem), (back, back_send)):
+            last = gone.at[pl.ds(0, 1)]
+            pltpu.make_async_copy(last, last, sem).wait()
+
+
+def finish(
+    back_hbm, gate_hbm, mg_hbm, mb_hbm, ow_hbm, ob_hbm, out_hbm,
+    back_in, gate, mg_ref, mb_ref, ow_ref, ob_ref, mixed, mgt, mbt, result, load_sem, out_sem,
+):
+    pieces = [
+        pltpu.make_async_copy(
+            back_hbm.at[pl.ds(i * 32, 32)], back_in.at[pl.ds(i * 32, 32)], load_sem.at[i]
+        )
+        for i in range(4)
+    ]
+    loads = [
+        pltpu.make_async_copy(src, dst, load_sem.at[4 + i])
+        for i, (src, dst) in enumerate(
+            (
+                (mg_hbm, mg_ref), (mb_hbm, mb_ref), (ow_hbm, ow_ref), (ob_hbm, ob_ref),
+                (gate_hbm, gate),
+            )
+        )
+    ]
+    for load in pieces + loads:
+        load.start()
+    for load in loads[:2]:
+        load.wait()
+    mgt[...] = column(mg_ref[...], 128)
+    mbt[...] = column(mb_ref[...], 128)
+    for load in pieces:
+        load.wait()
     values = back_in[...].astype(F32)
     center = values - jnp.mean(values, axis=0, keepdims=True)
     spread = jnp.mean(center * center, axis=0, keepdims=True)
     mixed[...] = (center * lax.rsqrt(spread + EPS)).reshape(1024, 128)
+    for load in loads[2:]:
+        load.wait()
     writes = []
     for t in range(8):
         norm = mixed[pl.ds(t, 128, stride=8), :] * mgt[...] + mbt[...]
@@ -322,16 +363,6 @@
 
     for write in writes:
         write.wait()
-    swap.wait_send()
-    for gone, sem in ((send_l, send_sem), (send_r, send_sem), (back, back_send)):
-        most = gone.at[pl.ds(0, CHIPS - 1)]
-        pltpu.make_async_copy(most, most, sem).wait()
-
-    @pl.when(core != TO_CORE[3])
-    def _():
-        for gone, sem in ((send_r, send_sem), (back, back_send)):
-            last = gone.at[pl.ds(0, 1)]
-            pltpu.make_async_copy(last, last, sem).wait()
 
 
 def per_device(
@@ -340,11 +371,15 @@
 ):
     dma = pltpu.SemaphoreType.DMA
     vmem = pltpu.VMEM
-    out = pl.pallas_call(
+    params = dict(has_side_effects=True, vmem_limit_bytes=56 << 20)
+    blocks, gate = pl.pallas_call(
         kernel,
-        out_shape=jax.ShapeDtypeStruct((4, 8, 32, 128), BF16),
-        in_specs=[pl.BlockSpec(memory_space=pl.ANY)] * 11,
-        out_specs=pl.BlockSpec(memory_space=pl.ANY),
+        out_shape=[
+            jax.ShapeDtypeStruct((CHIPS, 8, 128), BF16),
+            jax.ShapeDtypeStruct((1024, 128), F32),
+        ],
+        in_specs=[pl.BlockSpec(memory_space=pl.ANY)] * 7,
+        out_specs=[pl.BlockSpec(memory_space=pl.ANY)] * 2,
         scratch_shapes=[
             vmem((1024, 128), BF16),
             vmem((1, 128), F32),
@@ -353,11 +388,7 @@
             vmem((1, 512), F32),
             vmem((128, 128), BF16),
             vmem((1, 128), F32),
-            vmem((1, 128), F32),
-            vmem((1, 128), F32),
-            vmem((128, 128), BF16),
-            vmem((1, 128), F32),
-            dma((11,)),
+            dma((7,)),
             vmem((1024, 128), BF16),
             vmem((512, 128), BF16),
             vmem((512, 128), F32),
@@ -373,17 +404,10 @@
             vmem((2, 512, 128), BF16),
             vmem((2, 512, 128), F32),
             vmem((CHIPS, 8, 128), BF16),
-            vmem((CHIPS, 8, 128), BF16),
             vmem((1024, 128), F32),
-            vmem((1024, 128), F32),
-            vmem((128, 128), F32),
-            vmem((128, 128), F32),
-            vmem((4, 8, 32, 128), BF16),
-            dma, dma, dma((2,)), dma, dma, dma, dma, dma((4,)), pltpu.SemaphoreType.REGULAR,
+            dma, dma, dma((2,)), dma, dma, dma, dma, dma, pltpu.SemaphoreType.REGULAR,
         ],
-        compiler_params=pltpu.CompilerParams(
-            collective_id=0, has_side_effects=True, vmem_limit_bytes=56 << 20
-        ),
+        compiler_params=pltpu.CompilerParams(collective_id=0, **params),
         cost_estimate=pl.CostEstimate(
             flops=500_000_000, bytes_accessed=2_000_000, transcendentals=1_000_000
         ),
@@ -396,11 +420,29 @@
         proj_bias.reshape(1, -1),
         gate_weight,
         gate_bias.reshape(1, -1),
-        mid_gain.reshape(1, -1),
-        mid_bias.reshape(1, -1),
-        out_weight,
-        out_bias.reshape(1, -1),
     )
+    out = pl.pallas_call(
+        finish,
+        out_shape=jax.ShapeDtypeStruct((4, 8, 32, 128), BF16),
+        in_specs=[pl.BlockSpec(memory_space=pl.ANY)] * 6,
+        out_specs=pl.BlockSpec(memory_space=pl.ANY),
+        scratch_shapes=[
+            vmem((CHIPS, 8, 128), BF16),
+            vmem((1024, 128), F32),
+            vmem((1, 128), F32),
+            vmem((1, 128), F32),
+            vmem((128, 128), BF16),
+            vmem((1, 128), F32),
+            vmem((1024, 128), F32),
+            vmem((128, 128), F32),
+            vmem((128, 128), F32),
+            vmem((4, 8, 32, 128), BF16),
+            dma((9,)),
+            dma((4,)),
+        ],
+        compiler_params=pltpu.CompilerParams(vmem_limit_bytes=56 << 20),
+        name="finish",
+    )(blocks, gate, mid_gain.reshape(1, -1), mid_bias.reshape(1, -1), out_weight, out_bias.reshape(1, -1))
     return out.reshape(32, 32, 128)
 
 

time: 40.3 us -> 39.9 us (0.990)
  local copies, waits for them, and re-layouts: 1.67 us -> 0 us
  Pallas kernels: 38.5 us -> 39.8 us
    unnamed x1 -> x0, local copies, waits for them, and re-layouts: 1.67 us -> none
    pallas_call x1 -> x2, Pallas kernels: 38.5 us -> 39.8 us  [the longest x1 37.5 us: per_device(): pl.pallas_call(kernel, out_shape=[jax.ShapeDtypeStruct((CHIPS, 8, 128), B...]
where the time goes in v4:
time: 39.9 us; the launch traced here: 39.8 us
  Pallas kernels  39.8 us (100%)
    pallas_call x1, Pallas kernels, per_device(): pl.pallas_call(kernel, out_shape=[jax.ShapeDtypeStruct((CHIPS, 8, 128), B...  37.5 us
    pallas_call x1, Pallas kernels, per_device(): pl.pallas_call(finish, out_shape=jax.ShapeDtypeStruct((4, 8, 32, 128), BF...  2.28 us

profile of v4, /device:TPU:1, one launch (start us, length us, event | category | flops | bytes accessed | tf_op | source)
XLA Modules:
  0.0 39.8 jit_solution(18167954039741753448)
XLA Ops:
  0.0 37.5 %triangle.1 = (bf16[128,8,128]{2,1,0:T(8,128)(2,1)}, f32[1024,128]{1,0:T(8,128)}) custom-call(bf16[1024,128]{1,0:T(8,128)(2,1)} %bitcast.12, f32[1,128]{1,0:T(1,128)} %bitcast.14, f32[1,128]{1,0:T(1,128)} %bitcast.15, bf16[128,512]{1,0:T(8,128)(2,1)} %pw_hbm.1, f32[1,512]{1,0:T(1,128)} %bitcast.13, bf16[128,128]{1,0:T(8,128)(2,1)} %gw_hbm.1, f32[1,128]{1,0:T(1,128)} %bitcast.16), custom_call_target="tpu_custom_call" | custom-call | flops 500000000 | bytes 2000000 | tf_op jit(solution)/shard_map/triangle/pallas_call | solution.py:375
  37.5 2.3 %finish.1 = bf16[4,8,32,128]{3,2,1,0:T(8,128)(2,1)} custom-call(bf16[128,8,128]{2,1,0:T(8,128)(2,1)} %get-tuple-element.7.back_hbm, f32[1024,128]{1,0:T(8,128)} %get-tuple-element.8.gate_hbm, f32[1,128]{1,0:T(1,128)} %bitcast.9, f32[1,128]{1,0:T(1,128)} %bitcast.10, bf16[128,128]{1,0:T(8,128)(2,1)} %ow_hbm.1, f32[1,128]{1,0:T(1,128)} %bitcast.11), custom_call_target="tpu_custom_call" | custom-call | tf_op jit(solution)/shard_map/finish/pallas_call | solution.py:424

commit v5 on v4

--- a/solution.py
+++ b/solution.py
@@ -80,8 +80,9 @@
     partner = device(x, y, z, 1 - core)
     x_lo, x_hi = lax.rem(x, 2), lax.div(x, 2)
 
-    def send_waves(act):
-        for w, wave in enumerate(WAVES):
+    def send_waves(act, waves=(0, 1, 2, 3)):
+        for w in waves:
+            wave = WAVES[w]
             chips = []
             for hi, d in wave:
                 txh, tz = lax.rem(x_hi + hi, 2), lax.rem(z + d, NZ)
@@ -184,9 +185,9 @@
         else:
             pl.when(jnp.logical_not(jnp.logical_and(mine, core == TO_CORE[w])))(go)
 
-    send_waves(push_left)
+    send_waves(push_left, (0, 1, 3, 2))
     pl.semaphore_wait(mate_sem, 1)
-    send_waves(push_right)
+    send_waves(push_right, (2, 3, 0, 1))
     recv_l[slot] = send_l[chan]
 
     @pl.when(core == TO_CORE[3])
@@ -288,10 +289,10 @@
             hi, d = jnp.where(core == 0, hi0, hi1), jnp.where(core == 0, d0, d1)
             cols_of.append(lax.rem(x_hi + hi, 2) * NZ + lax.rem(z + NZ - d, NZ))
         came_from.append(cols_of)
+    multiply(1)
+    give(1)
     multiply(0)
     give(0)
-    multiply(1)
-    give(1)
 
     pltpu.make_async_copy(back_in, back_in, back_recv).wait()
 

time: 39.9 us -> 38.9 us (0.975)
  Pallas kernels: 39.8 us -> 38.7 us
    pallas_call x1, Pallas kernels: 37.5 us -> 36.4 us  [per_device(): pl.pallas_call(kernel, out_shape=[jax.ShapeDtypeStruct((CHIPS, 8, 128), B...]
where the time goes in v5:
time: 38.9 us; the launch traced here: 38.7 us
  Pallas kernels  38.7 us (99%)
    pallas_call x1, Pallas kernels, per_device(): pl.pallas_call(kernel, out_shape=[jax.ShapeDtypeStruct((CHIPS, 8, 128), B...  36.4 us
    pallas_call x1, Pallas kernels, per_device(): pl.pallas_call(finish, out_shape=jax.ShapeDtypeStruct((4, 8, 32, 128), BF...  2.28 us

profile of v5, /device:TPU:1, one launch (start us, length us, event | category | flops | bytes accessed | tf_op | source)
XLA Modules:
  0.0 38.7 jit_solution(15084852034921513231)
XLA Ops:
  0.0 36.4 %triangle.1 = (bf16[128,8,128]{2,1,0:T(8,128)(2,1)}, f32[1024,128]{1,0:T(8,128)}) custom-call(bf16[1024,128]{1,0:T(8,128)(2,1)} %bitcast.12, f32[1,128]{1,0:T(1,128)} %bitcast.14, f32[1,128]{1,0:T(1,128)} %bitcast.15, bf16[128,512]{1,0:T(8,128)(2,1)} %pw_hbm.1, f32[1,512]{1,0:T(1,128)} %bitcast.13, bf16[128,128]{1,0:T(8,128)(2,1)} %gw_hbm.1, f32[1,128]{1,0:T(1,128)} %bitcast.16), custom_call_target="tpu_custom_call" | custom-call | flops 500000000 | bytes 2000000 | tf_op jit(solution)/shard_map/triangle/pallas_call | solution.py:376
  36.4 2.3 %finish.1 = bf16[4,8,32,128]{3,2,1,0:T(8,128)(2,1)} custom-call(bf16[128,8,128]{2,1,0:T(8,128)(2,1)} %get-tuple-element.7.back_hbm, f32[1024,128]{1,0:T(8,128)} %get-tuple-element.8.gate_hbm, f32[1,128]{1,0:T(1,128)} %bitcast.9, f32[1,128]{1,0:T(1,128)} %bitcast.10, bf16[128,128]{1,0:T(8,128)(2,1)} %ow_hbm.1, f32[1,128]{1,0:T(1,128)} %bitcast.11), custom_call_target="tpu_custom_call" | custom-call | tf_op jit(solution)/shard_map/finish/pallas_call | solution.py:425

commit v6 on v5

--- a/solution.py
+++ b/solution.py
@@ -58,7 +58,7 @@
     x_hbm, ng_hbm, nb_hbm, pw_hbm, pb_hbm, gw_hbm, gb_hbm,
     back_in, gate_hbm,
     x_ref, ng_ref, nb_ref, pw_ref, pb_ref, gw_ref, gb_ref, load_sem,
-    xn, wt, pbt, grp_l, grp_r, send_l, send_r, recv_l, mate_l, recv_r, left, left_t, right, total,
+    xn, wt, pbt, grp_l, grp_r, send_l, send_r, recv_l, mate_l, recv_r, left, left_t, right,
     back, gate,
     send_sem, left_sem, right_sem, mate_send, mate_recv, back_send, back_recv, out_sem, mate_sem,
 ):
@@ -245,16 +245,15 @@
         pltpu.make_async_copy(arrived, arrived, right_sem.at[j]).wait()
         for half, source in enumerate((recv_r.at[core], recv_r.at[1 - core])):
             regroup(source, came_from[j], right.at[j], half * 256, 0)
-        total[j] = jnp.dot(left_t[...], right[j], preferred_element_type=F32)
-
-    def give(j):
+        return jnp.dot(left_t[...], right[j], preferred_element_type=F32)
+
+    def give(j, product):
         places = []
         for i in range(16):
             row = ROWS[i]
             tiles = []
             for q in range(4):
-                here = pl.ds(row * 32 + q * 8, 8)
-                tiles.append(total[j, here, :])
+                tiles.append(product[row * 32 + q * 8 : row * 32 + q * 8 + 8])
             for m, tile in enumerate(transpose_blocks(tiles, lane8)):
                 place_in = j * 64 + i * 4 + m
                 back[place_in] = tile.astype(BF16)
@@ -289,10 +288,8 @@
             hi, d = jnp.where(core == 0, hi0, hi1), jnp.where(core == 0, d0, d1)
             cols_of.append(lax.rem(x_hi + hi, 2) * NZ + lax.rem(z + NZ - d, NZ))
         came_from.append(cols_of)
-    multiply(1)
-    give(1)
-    multiply(0)
-    give(0)
+    give(1, multiply(1))
+    give(0, multiply(0))
 
     pltpu.make_async_copy(back_in, back_in, back_recv).wait()
 
@@ -403,7 +400,6 @@
             vmem((512, 512), BF16),
             vmem((512, 512), BF16),
             vmem((2, 512, 128), BF16),
-            vmem((2, 512, 128), F32),
             vmem((CHIPS, 8, 128), BF16),
             vmem((1024, 128), F32),
             dma, dma, dma((2,)), dma, dma, dma, dma, dma, pltpu.SemaphoreType.REGULAR,

time: 38.9 us -> 38.9 us (level)
  no operation moved by 1% of the time
where the time goes in v6:
time: 38.9 us; the launch traced here: 38.7 us
  Pallas kernels  38.7 us (99%)
    pallas_call x1, Pallas kernels, per_device(): pl.pallas_call(kernel, out_shape=[jax.ShapeDtypeStruct((CHIPS, 8, 128), B...  36.4 us
    pallas_call x1, Pallas kernels, per_device(): pl.pallas_call(finish, out_shape=jax.ShapeDtypeStruct((4, 8, 32, 128), BF...  2.28 us

profile of v6, /device:TPU:1, one launch (start us, length us, event | category | flops | bytes accessed | tf_op | source)
XLA Modules:
  0.0 38.7 jit_solution(12626378646342398918)
XLA Ops:
  0.0 36.4 %triangle.1 = (bf16[128,8,128]{2,1,0:T(8,128)(2,1)}, f32[1024,128]{1,0:T(8,128)}) custom-call(bf16[1024,128]{1,0:T(8,128)(2,1)} %bitcast.12, f32[1,128]{1,0:T(1,128)} %bitcast.14, f32[1,128]{1,0:T(1,128)} %bitcast.15, bf16[128,512]{1,0:T(8,128)(2,1)} %pw_hbm.1, f32[1,512]{1,0:T(1,128)} %bitcast.13, bf16[128,128]{1,0:T(8,128)(2,1)} %gw_hbm.1, f32[1,128]{1,0:T(1,128)} %bitcast.16), custom_call_target="tpu_custom_call" | custom-call | flops 500000000 | bytes 2000000 | tf_op jit(solution)/shard_map/triangle/pallas_call | solution.py:373
  36.4 2.3 %finish.1 = bf16[4,8,32,128]{3,2,1,0:T(8,128)(2,1)} custom-call(bf16[128,8,128]{2,1,0:T(8,128)(2,1)} %get-tuple-element.7.back_hbm, f32[1024,128]{1,0:T(8,128)} %get-tuple-element.8.gate_hbm, f32[1,128]{1,0:T(1,128)} %bitcast.9, f32[1,128]{1,0:T(1,128)} %bitcast.10, bf16[128,128]{1,0:T(8,128)(2,1)} %ow_hbm.1, f32[1,128]{1,0:T(1,128)} %bitcast.11), custom_call_target="tpu_custom_call" | custom-call | tf_op jit(solution)/shard_map/finish/pallas_call | solution.py:421
